TPU v7x, 512 devices: a whole 4x8x8 slice. The times are simulated.
512 devices in a mesh: row: 8 (over z), col: 64 (over x, y, core).
Axes of the slice: x: 4, y: 8, z: 8, core: 2. Of those that a mesh axis runs over, the one named last changes fastest.
Arguments:
- top_multipoles: bfloat16 [2048, 256], P('row'), may hold values from -6 to 6
- coarse_multipoles: bfloat16 [16384, 256], P(('row', 'col')), may hold values from -6 to 6
- fine_multipoles: bfloat16 [131072, 256], P(('row', 'col')), may hold values from -6 to 6
- m2l_ops: bfloat16 [16, 256, 256], replicated, may hold values from -0.09375 to 0.09375
- l2l_ops: bfloat16 [8, 256, 256], replicated, may hold values from -0.375 to 0.375
- top_source: int32 [512, 16, 24], P(('row', 'col')), may hold values from 0 to 2047, as said below
- top_target: int32 [512, 16, 24], P(('row', 'col')), may hold values from 0 to 256, as said below
- coarse_source: int32 [512, 16, 96], P(('row', 'col')), may hold values from 0 to 16383, as said below
- coarse_target: int32 [512, 16, 96], P(('row', 'col')), may hold values from 0 to 32, as said below
- fine_source: int32 [512, 16, 384], P(('row', 'col')), may hold values from 0 to 767, as said below
- fine_target: int32 [512, 16, 384], P(('row', 'col')), may hold values from 0 to 256, as said below
Outputs:
- fine_local: float32 [131072, 256], P(('row', 'col'))
Inputs may be any that keep to these rules, and one draw needn't show every extreme that they name: `top_source`: A slot of device d in coarse segment g = d // 64 names a source in [(g - 1) * 256, (g + 2) * 256). `top_target`: the value 256 marks an empty slot. `coarse_source`: A slot of device d names a source in [(d - 1) * 32, (d + 2) * 32). `coarse_target`: the value 32 marks an empty slot. A slot of device d names the finest-level box (d - 1) * 256 + fine_source, which lies in [0, 131072). `fine_target`: the value 256 marks an empty slot.
All inputs are finite; a program needn't handle non-finite values.
Results may differ from a plain program's by a relative error of at most 0.0034.
Values may be sent and summed in bfloat16 or wider, within the bound.
A program may use at most 64 MiB of HBM per device.

v0:
```python
import jax
import jax.numpy as jnp
from jax import lax
from jax.sharding import PartitionSpec as P


def padded(block, sides, width):
    for axis, dim in sides:
        count = lax.axis_size(axis)
        forward = [(i, i + 1) for i in range(count - 1)]
        backward = [(target, source) for source, target in forward]
        low = lax.ppermute(
            lax.slice_in_dim(block, block.shape[dim] - width, None, axis=dim), axis, forward
        )
        high = lax.ppermute(lax.slice_in_dim(block, 0, width, axis=dim), axis, backward)
        block = jnp.concatenate([low, block, high], axis=dim)
    return block


def spread(window, src, tgt, ops, count):
    width = window.shape[0]
    win_rows = jnp.arange(width, dtype=jnp.int32)
    out_rows = jnp.arange(count, dtype=jnp.int32)

    def turn(r, acc):
        picker = (src[r][:, None] == win_rows[None, :]).astype(jnp.bfloat16)
        rows = jnp.dot(picker, window, preferred_element_type=jnp.float32).astype(jnp.bfloat16)
        prod = jnp.dot(rows, ops[r], preferred_element_type=jnp.float32)
        placer = (out_rows[:, None] == tgt[r][None, :]).astype(jnp.float32)
        return acc + jnp.dot(
            placer, prod, preferred_element_type=jnp.float32, precision=lax.Precision.HIGHEST
        )

    start = jnp.zeros((count, window.shape[1]), jnp.float32)
    return lax.fori_loop(0, ops.shape[0], turn, start)


def descend(parents, l2l_ops):
    child = jnp.einsum("pd,ode->poe", parents, l2l_ops, preferred_element_type=jnp.float32)
    return child.reshape(-1, parents.shape[1])


def per_device(
    top_multipoles,
    coarse_multipoles,
    fine_multipoles,
    m2l_ops,
    l2l_ops,
    top_source,
    top_target,
    coarse_source,
    coarse_target,
    fine_source,
    fine_target,
):
    group_boxes = top_multipoles.shape[0]
    share = group_boxes // lax.axis_size("col")
    top_window = padded(top_multipoles, (("row", 0),), group_boxes)
    row_base = (lax.axis_index("row") - 1) * group_boxes
    top_full = spread(top_window, top_source[0] - row_base, top_target[0], m2l_ops, group_boxes)
    summed = lax.psum(top_full, "col")
    own_top = lax.dynamic_slice_in_dim(summed, lax.axis_index("col") * share, share, 0)
    device = lax.axis_index(("row", "col"))
    coarse_boxes = coarse_multipoles.shape[0]
    coarse_window = padded(coarse_multipoles, ((("row", "col"), 0),), coarse_boxes)
    coarse_sum = descend(own_top.astype(jnp.bfloat16), l2l_ops) + spread(
        coarse_window,
        coarse_source[0] - (device - 1) * coarse_boxes,
        coarse_target[0],
        m2l_ops,
        coarse_boxes,
    )
    coarse_local = coarse_sum.astype(jnp.bfloat16)
    fine_boxes = fine_multipoles.shape[0]
    fine_window = padded(fine_multipoles, ((("row", "col"), 0),), fine_boxes)
    return descend(coarse_local, l2l_ops) + spread(
        fine_window, fine_source[0], fine_target[0], m2l_ops, fine_boxes
    )


def solution(mesh):
    in_specs = (
        P("row", None),
        P(("row", "col"), None),
        P(("row", "col"), None),
        P(),
        P(),
        P(("row", "col"), None, None),
        P(("row", "col"), None, None),
        P(("row", "col"), None, None),
        P(("row", "col"), None, None),
        P(("row", "col"), None, None),
        P(("row", "col"), None, None),
    )
    out_specs = P(("row", "col"), None)
    return jax.shard_map(
        per_device, mesh=mesh, in_specs=in_specs, out_specs=out_specs, check_vma=False
    )
```

profile of v0, /device:TPU:192, one launch (start us, length us, event | category | flops | bytes accessed | tf_op | source)
XLA Modules:
  0.0 397.4 jit_solution(14145473161494269832)
XLA Ops:
  0.0 6.2 %collective-permute-start.5 = (bf16[256,256]{1,0:T(8,128)(2,1)}, bf16[256,256]{1,0:T(8,128)(2,1)S(1)}, u32[]{:S(2)}, u32[]{:S(2)}) collective-permute-start(bf16[256,256]{1,0:T(8,128)(2,1)} %param.19), channel_id=1, source_target_pairs={{1,0},{2,1},{3,2},{4,3},{5,4},{6,5},{7,6},{8,7},{9,8},{10,9},{11,1... | collective-permute-start | bytes 393224 | tf_op jit(solution)/shard_map/ppermute | solution.py:15
  6.2 1.9 collective-permute-start.4
  8.2 7.9 %collective-permute-start.3 = (bf16[32,256]{1,0:T(8,128)(2,1)}, bf16[32,256]{1,0:T(8,128)(2,1)S(1)}, u32[]{:S(2)}, u32[]{:S(2)}) collective-permute-start(bf16[32,256]{1,0:T(8,128)(2,1)} %param.18), channel_id=1, source_target_pairs={{1,0},{2,1},{3,2},{4,3},{5,4},{6,5},{7,6},{8,7},{9,8},{10,9},{11,1... | collective-permute-start | bytes 49160 | tf_op jit(solution)/shard_map/ppermute | solution.py:15
  16.0 1.9 collective-permute-start.2
  18.0 1.9 collective-permute-start.1
  21.3 6.7 %collective-permute-start = (bf16[256,256]{1,0:T(8,128)(2,1)}, bf16[256,256]{1,0:T(8,128)(2,1)S(1)}, u32[]{:S(2)}, u32[]{:S(2)}) collective-permute-start(bf16[256,256]{1,0:T(8,128)(2,1)} %param.17), channel_id=1, source_target_pairs={{0,64},{64,128},{128,192},{192,256},{256,320},{320,384},{384,448},... | collective-permute-start | bytes 393224 | tf_op jit(solution)/shard_map/ppermute | solution.py:12
  28.7 33.8 %while.43 = (s32[]{:T(128)}, f32[32,256]{1,0:T(8,128)S(1)}, s32[16,96]{1,0:T(8,128)}, s32[16,96]{1,0:T(8,128)S(1)}, bf16[96,256]{1,0:T(8,128)(2,1)S(1)}, /*index...) while((s32[]{:T(128)}, f32[32,256]{1,0:T(8,128)S(1)}, s32[16,96]{1,0:T(8,128)}, ...), condition=%wide.region_4.0_spmd.clone, body=%wide.region_3.0_spmd.clone.sunk | while | flops 26791936 | bytes 444783 | solution.py:35
  62.6 43.4 %while.44 = (s32[]{:T(128)}, f32[256,256]{1,0:T(8,128)S(1)}, s32[16,384]{1,0:T(8,128)}, s32[16,384]{1,0:T(8,128)}, bf16[768,256]{1,0:T(8,128)(2,1)S(1)}, /*index...) while((s32[]{:T(128)}, f32[256,256]{1,0:T(8,128)S(1)}, s32[16,384]{1,0:T(8,128)}, ...), condition=%wide.region_6.0_spmd.clone, body=%wide.region_5.0_spmd.clone.sunk | while | flops 503939072 | bytes 1844335 | solution.py:35
  63.4 1.4 fusion.82
  66.1 1.4 fusion.82
  68.9 1.4 fusion.82
  71.6 1.4 fusion.82
  74.3 1.4 fusion.82
  77.0 1.4 fusion.82
  79.7 1.4 fusion.82
  82.4 1.4 fusion.82
  85.1 1.4 fusion.82
  87.8 1.4 fusion.82
  96.0 1.4 fusion.82
  98.7 1.4 fusion.82
  101.4 1.4 fusion.82
  104.1 1.4 fusion.82
  106.1 36.5 %while.42 = (s32[]{:T(128)}, f32[256,256]{1,0:T(8,128)S(1)}, s32[16,24]{1,0:T(8,128)}, s32[16,24]{1,0:T(8,128)S(1)}, bf16[768,256]{1,0:T(8,128)(2,1)S(1)}, /*ind...) while((s32[]{:T(128)}, f32[256,256]{1,0:T(8,128)S(1)}, s32[16,24]{1,0:T(8,128)}, ...), condition=%wide.region_1.0_spmd.clone, body=%wide.region_0.0_spmd.clone.sunk | while | flops 31619076 | bytes 1098415 | solution.py:35
  142.7 253.3 %all-reduce.1 = bf16[256,256]{1,0:T(8,128)(2,1)S(1)} all-reduce(f32[256,256]{1,0:T(8,128)S(1)} %get-tuple-element.422), channel_id=1, replica_groups=mesh['row'=8,'col'=64] {'col'}, use_global_device_ids=true, to_apply=%region_2.0 | all-reduce | flops 65536 | bytes 393216 | tf_op jit(solution)/shard_map/psum | solution.py:61
  (153 shorter events, 95.8 us)
Async XLA Ops:
  0.0 396.0 %copy-start = (bf16[8,256,256]{2,1,0:T(8,128)(2,1)S(1)}, bf16[8,256,256]{2,1,0:T(8,128)(2,1)}, u32[]{:S(2)}) copy-start(bf16[8,256,256]{2,1,0:T(8,128)(2,1)} %param.21) | copy-start | bytes 3145732
  0.0 62.6 %copy-start.1 = (bf16[256,256]{1,0:T(8,128)(2,1)S(1)}, bf16[256,256]{1,0:T(8,128)(2,1)}, u32[]{:S(2)}) copy-start(bf16[256,256]{1,0:T(8,128)(2,1)} %param.19) | copy-start | bytes 393220
  0.0 62.6 %collective-permute-start.5 = (bf16[256,256]{1,0:T(8,128)(2,1)}, bf16[256,256]{1,0:T(8,128)(2,1)S(1)}, u32[]{:S(2)}, u32[]{:S(2)}) collective-permute-start(bf16[256,256]{1,0:T(8,128)(2,1)} %param.19), channel_id=1, source_target_pairs={{1,0},{2,1},{3,2},{4,3},{5,4},{6,5},{7,6},{8,7},{9,8},{10,9},{11,1... | collective-permute-start | bytes 393224 | tf_op jit(solution)/shard_map/ppermute | solution.py:15
  6.2 56.3 %collective-permute-start.4 = (bf16[256,256]{1,0:T(8,128)(2,1)}, bf16[256,256]{1,0:T(8,128)(2,1)S(1)}, u32[]{:S(2)}, u32[]{:S(2)}) collective-permute-start(bf16[256,256]{1,0:T(8,128)(2,1)} %param.19), channel_id=1, source_target_pairs={{0,1},{1,2},{2,3},{3,4},{4,5},{5,6},{6,7},{7,8},{8,9},{9,10},{10,1... | collective-permute-start | bytes 393224 | tf_op jit(solution)/shard_map/ppermute | solution.py:12
  8.2 13.1 %collective-permute-start.3 = (bf16[32,256]{1,0:T(8,128)(2,1)}, bf16[32,256]{1,0:T(8,128)(2,1)S(1)}, u32[]{:S(2)}, u32[]{:S(2)}) collective-permute-start(bf16[32,256]{1,0:T(8,128)(2,1)} %param.18), channel_id=1, source_target_pairs={{1,0},{2,1},{3,2},{4,3},{5,4},{6,5},{7,6},{8,7},{9,8},{10,9},{11,1... | collective-permute-start | bytes 49160 | tf_op jit(solution)/shard_map/ppermute | solution.py:15
  16.0 12.0 %collective-permute-start.2 = (bf16[32,256]{1,0:T(8,128)(2,1)}, bf16[32,256]{1,0:T(8,128)(2,1)S(1)}, u32[]{:S(2)}, u32[]{:S(2)}) collective-permute-start(bf16[32,256]{1,0:T(8,128)(2,1)} %param.18), channel_id=1, source_target_pairs={{0,1},{1,2},{2,3},{3,4},{4,5},{5,6},{6,7},{7,8},{8,9},{9,10},{10,1... | collective-permute-start | bytes 49160 | tf_op jit(solution)/shard_map/ppermute | solution.py:12
  18.0 88.1 %collective-permute-start.1 = (bf16[256,256]{1,0:T(8,128)(2,1)}, bf16[256,256]{1,0:T(8,128)(2,1)S(1)}, u32[]{:S(2)}, u32[]{:S(2)}) collective-permute-start(bf16[256,256]{1,0:T(8,128)(2,1)} %param.17), channel_id=1, source_target_pairs={{64,0},{128,64},{192,128},{256,192},{320,256},{384,320},{448,384},... | collective-permute-start | bytes 393224 | tf_op jit(solution)/shard_map/ppermute | solution.py:15
  21.3 84.8 %collective-permute-start = (bf16[256,256]{1,0:T(8,128)(2,1)}, bf16[256,256]{1,0:T(8,128)(2,1)S(1)}, u32[]{:S(2)}, u32[]{:S(2)}) collective-permute-start(bf16[256,256]{1,0:T(8,128)(2,1)} %param.17), channel_id=1, source_target_pairs={{0,64},{64,128},{128,192},{192,256},{256,320},{320,384},{384,448},... | collective-permute-start | bytes 393224 | tf_op jit(solution)/shard_map/ppermute | solution.py:12
  62.6 43.5 %copy-start.2 = (bf16[256,256]{1,0:T(8,128)(2,1)S(1)}, bf16[256,256]{1,0:T(8,128)(2,1)}, u32[]{:S(2)}) copy-start(bf16[256,256]{1,0:T(8,128)(2,1)} %param.17) | copy-start | bytes 393220
where the time goes:
time: 401 us; the launch traced here: 397 us
  blocking collectives  253 us (63%)
  matrix products  78.6 us (20%)
  local copies, waits for them, and re-layouts  34.3 us (9%)
  starting transfers between devices  26.5 us (7%)
    psum x1, blocking collectives, per_device(): summed = lax.psum(top_full, 'col')  253 us
    dot_general x48, matrix products, turn(): prod = jnp.dot(rows, ops[r], preferred_element_type=jnp.float32)  62.1 us
    eq x32, local copies, waits for them, and re-layouts, turn(): placer = (out_rows[:, None] == tgt[r][None, :]).astype(jnp.float32)  22.3 us
    dot_general x48, matrix products, turn(): jnp.dot(placer, prod, preferred_element_type=jnp.float32, precision=lax.P...  16.1 us
    ppermute x3, starting transfers between devices, padded(): lax.ppermute(lax.slice_in_dim(block, 0, width, axis=dim), axis, backward)  16 us
    dynamic_slice x16, local copies, waits for them, and re-layouts, turn(): picker = (src[r][:, None] == win_rows[None, :]).astype(jnp.bfloat16)  12 us
    ppermute x3, starting transfers between devices, padded(): lax.ppermute(lax.slice_in_dim(block, block.shape[dim] - width, None, axis...  10.5 us
  transfers between devices with their start and end apart: 6, of which 0 were waited for; matrix products, arithmetic and copies ran while one was open for 20% of the time, Pallas kernels for 0%

commit v1 on v0

v1 whole, which is shorter than its diff:
```python
import functools

import jax
import jax.numpy as jnp
from jax import lax
from jax.experimental import pallas as pl
from jax.experimental.pallas import tpu as pltpu
from jax.sharding import PartitionSpec as P

CORES = 2
XS = 4
MESH = pl.DeviceIdType.MESH
BF = jnp.bfloat16
F32 = jnp.float32


def onehot(rows, picks):
    number = lax.broadcasted_iota(jnp.int32, (rows, picks.shape[1]), 0)
    return jnp.where(number == picks, 1.0, 0.0).astype(BF)


def dot(a, b):
    return jnp.dot(a, b, preferred_element_type=F32)


def dot_nt(a, b):
    return lax.dot_general(a, b, (((1,), (1,)), ((), ())), preferred_element_type=F32)


def split(a):
    hi = a.astype(BF)
    return hi, (a - hi.astype(F32)).astype(BF)


def children(parents, ops):
    n, c = parents.shape
    octants, depth, _ = ops.shape
    rep = jnp.broadcast_to(parents[:, None, :], (n, octants, c)).reshape(n * octants, c)
    which = lax.broadcasted_iota(jnp.int32, (n, octants, c), 1).reshape(n * octants, c)
    parts = [jnp.where(which == o, rep, 0.0).astype(BF) for o in range(octants)]
    return dot(jnp.concatenate(parts, axis=1), ops.reshape(octants * depth, c))


def kernel(
    n_row,
    n_col,
    top_ref,
    coarse_ref,
    fine_ref,
    m2l_ref,
    l2l_ref,
    tsrc_ref,
    ttgt_ref,
    csrc_ref,
    ctgt_ref,
    fsrc_ref,
    ftgt_ref,
    out_ref,
    twin,
    cwin,
    fwin,
    ops,
    l2l,
    tsrc,
    ttgt,
    csrc,
    ctgt,
    fsrc,
    ftgt,
    square,
    mine,
    lists,
    tpick,
    cpick,
    ctop,
    ccoarse,
    cfine,
    atop,
    acoarse,
    acc,
    outbox,
    inbox,
    local_sem,
    wsend,
    wrecv,
    lsend,
    lrecv,
    rsend,
    rrecv,
):
    classes, coeffs = m2l_ref.shape[0], m2l_ref.shape[1]
    seg = top_ref.shape[0]
    half = seg // CORES
    quarter = seg // XS
    cb, b = coarse_ref.shape[0], fine_ref.shape[0]
    capt = tsrc_ref.shape[2]
    capc = csrc_ref.shape[2]
    ys = n_col // (XS * CORES)
    mates = XS * CORES
    planes = ys * CORES

    row, col = lax.axis_index("row"), lax.axis_index("col")
    x, j = col // planes, lax.rem(col, planes)
    y, core = j // CORES, lax.rem(col, CORES)
    device = row * n_col + col
    total = n_row * n_col

    def place(index):
        return (index // n_col, lax.rem(index, n_col))

    after = place(lax.rem(device + 1, total))
    before = place(lax.rem(device + total - 1, total))
    above = (lax.rem(row + 1, n_row), col)
    below = (lax.rem(row + n_row - 1, n_row), col)

    def mate(k):
        m = lax.rem(x * CORES + core + k, mates)
        return (row, (m // CORES) * planes + y * CORES + lax.rem(m, CORES))

    def peer(k):
        return (row, x * planes + lax.rem(j + k, planes))

    barrier = pltpu.get_barrier_semaphore()
    partners = [after, before, above, below]
    partners += [mate(k) for k in range(1, mates)]
    partners += [peer(k) for k in range(1, planes)]
    for partner in partners:
        pl.semaphore_signal(barrier, inc=1, device_id=partner, device_id_type=MESH)

    own_top = top_ref.at[pl.ds(pl.multiple_of(core * half, half), half)]
    moves = [
        (tsrc_ref, tsrc),
        (ttgt_ref, ttgt),
        (fsrc_ref, fsrc),
        (ftgt_ref, ftgt),
        (csrc_ref, csrc),
        (ctgt_ref, ctgt),
        (own_top, twin.at[pl.ds(half, half)]),
        (coarse_ref, cwin.at[pl.ds(cb, cb)]),
        (m2l_ref, ops),
        (fine_ref, fwin.at[pl.ds(b, b)]),
        (l2l_ref, l2l),
    ]
    moves = [pltpu.make_async_copy(s, d, local_sem.at[i]) for i, (s, d) in enumerate(moves)]
    for move in moves:
        move.start()

    square[...] = jnp.zeros_like(square)
    unused = lists.shape[0] - mates * capt
    lists[pl.ds(mates * capt, unused)] = jnp.full((unused, lists.shape[1]), -1, jnp.int32)
    moves[0].wait()
    moves[1].wait()
    square[pl.ds(0, classes), pl.ds(0, capt)] = tsrc[0]
    square[pl.ds(classes, classes), pl.ds(0, capt)] = ttgt[0]
    columns = square[...].T[:capt]
    mine[...] = columns
    lists[pl.ds(0, capt)] = columns

    pl.semaphore_wait(barrier, len(partners))

    def remote(src, dst, send, recv, to):
        return pltpu.make_async_remote_copy(
            src_ref=src, dst_ref=dst, send_sem=send, recv_sem=recv, device_id=to, device_id_type=MESH
        )

    windows = [
        (own_top, twin.at[pl.ds(0, half)], above),
        (own_top, twin.at[pl.ds(2 * half, half)], below),
        (coarse_ref, cwin.at[pl.ds(0, cb)], after),
        (coarse_ref, cwin.at[pl.ds(2 * cb, cb)], before),
        (fine_ref, fwin.at[pl.ds(0, b)], after),
        (fine_ref, fwin.at[pl.ds(2 * b, b)], before),
    ]
    windows = [remote(s, d, wsend.at[i], wrecv.at[i], to) for i, (s, d, to) in enumerate(windows)]
    posts = [
        remote(mine, lists.at[pl.ds(k * capt, capt)], lsend.at[k], lrecv.at[k], mate(k))
        for k in range(1, mates)
    ]
    for copy in windows[:2] + posts + windows[2:]:
        copy.start()

    for i in (2, 3, 4, 5):
        moves[i].wait()

    def fine_counts(r, _):
        targets = onehot(b, ftgt[0, pl.ds(r, 1), :])
        sources = onehot(3 * b, fsrc[0, pl.ds(r, 1), :])
        cfine[r] = dot_nt(targets, sources).astype(BF)
        return 0

    cpick[...] = jnp.full(cpick.shape, -1, jnp.int32)
    cpick[pl.ds(0, classes), pl.ds(0, capc)] = csrc[0] - (device - 1) * cb
    cpick[pl.ds(classes, classes), pl.ds(0, capc)] = ctgt[0]
    cwin[pl.ds(3 * cb, cwin.shape[0] - 3 * cb)] = jnp.zeros((cwin.shape[0] - 3 * cb, coeffs), BF)

    def coarse_counts(r, _):
        targets = onehot(cb, cpick[pl.ds(classes + r, 1), :])
        sources = onehot(cwin.shape[0], cpick[pl.ds(r, 1), :])
        ccoarse[pl.ds(pl.multiple_of(r * cb, cb), cb)] = dot_nt(targets, sources).astype(BF)
        return 0

    lax.fori_loop(0, classes, coarse_counts, 0)
    lax.fori_loop(0, classes // 2, fine_counts, 0)

    for copy in posts:
        copy.wait_recv()
    rows = lists[...].T[: 2 * classes]
    offset = rows[:classes] - (row - 1) * seg
    which = jnp.where(offset >= seg, 1, 0) + jnp.where(offset >= 2 * seg, 1, 0)
    inside = offset - which * seg - core * half
    inside = jnp.where((inside >= 0) & (inside < half), which * half + inside, -1)
    tpick[pl.ds(0, classes)] = inside
    tpick[pl.ds(classes, classes)] = rows[classes:] - x * quarter

    def top_counts(r, _):
        targets = onehot(quarter, tpick[pl.ds(classes + r, 1), :])
        sources = onehot(3 * half, tpick[pl.ds(r, 1), :])
        ctop[pl.ds(pl.multiple_of(r * quarter, quarter), quarter)] = dot_nt(targets, sources).astype(BF)
        return 0

    lax.fori_loop(0, classes, top_counts, 0)

    def class_columns(r):
        return pl.ds(pl.multiple_of(r * coeffs, coeffs), coeffs)

    moves[6].wait()
    windows[0].wait_recv()
    windows[1].wait_recv()

    def top_rows(r, _):
        counts = ctop[pl.ds(pl.multiple_of(r * quarter, quarter), quarter)]
        hi, lo = split(dot(counts, twin[...]))
        atop[pl.ds(0, quarter), class_columns(r)] = hi
        atop[pl.ds(quarter, quarter), class_columns(r)] = lo
        return 0

    lax.fori_loop(0, classes, top_rows, 0)
    moves[8].wait()
    part = dot(atop[...], ops[...].reshape(classes * coeffs, coeffs))
    part = part[:quarter] + part[quarter:]
    lanes = coeffs // 2
    left = part[:, :lanes].reshape(quarter // 8, 8, lanes)
    right = part[:, lanes:].reshape(quarter // 8, 8, lanes)
    low = lax.broadcasted_iota(jnp.int32, left.shape, 1) < 4
    even = jnp.where(low, left, pltpu.roll(right, 4, 1))
    odd = jnp.where(low, pltpu.roll(left, 4, 1), right)
    for i in range(quarter // 8):
        outbox[2 * i] = even[i]
        outbox[2 * i + 1] = odd[i]
    shares = [
        remote(outbox.at[lax.rem(j + k, planes)], inbox.at[k], rsend.at[k], rrecv.at[k], peer(k))
        for k in range(1, planes)
    ]
    for copy in shares:
        copy.start()
    inbox[0] = outbox[j]

    lax.fori_loop(classes // 2, classes, fine_counts, 0)

    for copy in windows[2:4]:
        copy.wait_recv()
    moves[7].wait()

    def coarse_rows(r, _):
        hi, lo = split(dot(ccoarse[pl.ds(pl.multiple_of(r * cb, cb), cb)], cwin[...]))
        acoarse[pl.ds(0, cb), class_columns(r)] = hi
        acoarse[pl.ds(cb, cb), class_columns(r)] = lo
        return 0

    lax.fori_loop(0, classes, coarse_rows, 0)
    middle = dot(acoarse[...], ops[...].reshape(classes * coeffs, coeffs))
    middle = middle[:cb] + middle[cb:]

    for copy in windows[4:]:
        copy.wait_recv()
    moves[9].wait()
    acc[...] = jnp.zeros_like(acc)

    def fine_rows(r, _):
        acc[...] += dot(dot(cfine[r], fwin[...]).astype(BF), ops[r])
        return 0

    lax.fori_loop(0, classes, fine_rows, 0)

    moves[10].wait()
    for copy in shares:
        copy.wait_recv()
    summed = inbox[0]
    for k in range(1, planes):
        summed += inbox[k]
    top = jnp.concatenate([summed[:4], summed[4:]], axis=1).astype(BF).astype(F32)
    coarse = children(top, l2l[...]) + middle
    coarse = coarse.astype(BF).astype(F32)
    out_ref[...] = children(coarse, l2l[...]) + acc[...]

    for copy in windows + posts + shares:
        copy.wait_send()


def solution(mesh):
    n_row, n_col = mesh.shape["row"], mesh.shape["col"]
    mates = XS * CORES
    planes = n_col // XS

    def per_device(*args):
        top, coarse, fine, m2l, l2l, tsrc, ttgt, csrc, ctgt, fsrc, ftgt = args
        classes, coeffs = m2l.shape[0], m2l.shape[1]
        seg, cb, b = top.shape[0], coarse.shape[0], fine.shape[0]
        quarter = seg // XS
        capt = tsrc.shape[2]
        pad = 128
        slots = -(-mates * capt // pad) * pad
        crows = -(-3 * cb // pad) * pad
        scratch = [
            pltpu.VMEM((3 * seg // CORES, coeffs), BF),
            pltpu.VMEM((crows, coeffs), BF),
            pltpu.VMEM((3 * b, coeffs), BF),
            pltpu.VMEM(m2l.shape, BF),
            pltpu.VMEM(l2l.shape, BF),
            *[pltpu.VMEM(a.shape, jnp.int32) for a in (tsrc, ttgt, csrc, ctgt, fsrc, ftgt)],
            pltpu.VMEM((pad, pad), jnp.int32),
            pltpu.VMEM((capt, pad), jnp.int32),
            pltpu.VMEM((slots, pad), jnp.int32),
            pltpu.VMEM((2 * classes, slots), jnp.int32),
            pltpu.VMEM((2 * classes, pad), jnp.int32),
            pltpu.VMEM((classes * quarter, 3 * seg // CORES), BF),
            pltpu.VMEM((classes * cb, crows), BF),
            pltpu.VMEM((classes, b, 3 * b), BF),
            pltpu.VMEM((2 * quarter, classes * coeffs), BF),
            pltpu.VMEM((2 * cb, classes * coeffs), BF),
            pltpu.VMEM((b, coeffs), F32),
            pltpu.VMEM((planes, 8, coeffs // 2), F32),
            pltpu.VMEM((planes, 8, coeffs // 2), F32),
            pltpu.SemaphoreType.DMA((11,)),
            pltpu.SemaphoreType.DMA((6,)),
            pltpu.SemaphoreType.DMA((6,)),
            pltpu.SemaphoreType.DMA((mates,)),
            pltpu.SemaphoreType.DMA((mates,)),
            pltpu.SemaphoreType.DMA((planes,)),
            pltpu.SemaphoreType.DMA((planes,)),
        ]
        return pl.pallas_call(
            functools.partial(kernel, n_row, n_col),
            out_shape=jax.ShapeDtypeStruct((b, coeffs), F32),
            in_specs=[pl.BlockSpec(memory_space=pl.ANY)] * len(args),
            out_specs=pl.BlockSpec(memory_space=pltpu.VMEM),
            scratch_shapes=scratch,
            compiler_params=pltpu.CompilerParams(
                collective_id=0, has_side_effects=True, vmem_limit_bytes=40 * 1024 * 1024
            ),
        )(*args)

    both = P(("row", "col"), None)
    lists = P(("row", "col"), None, None)
    in_specs = (P("row", None), both, both, P(), P()) + (lists,) * 6
    return jax.shard_map(per_device, mesh=mesh, in_specs=in_specs, out_specs=both, check_vma=False)
```

time: 401 us -> 49 us (0.12)
  the two profiles are of different devices: /device:TPU:192 before, /device:TPU:5 now
where the time goes in v1:
time: 49 us; the launch traced here: 48.4 us
  Pallas kernels  38.1 us (78%)
  local copies, waits for them, and re-layouts  10.3 us (21%)
    pallas_call x1, Pallas kernels, per_device(): pl.pallas_call(functools.partial(kernel, n_row, n_col), out_shape=jax.Sha...  38.1 us
    unnamed x23, local copies, waits for them, and re-layouts  10.3 us

profile of v1, /device:TPU:5, one launch (start us, length us, event | category | flops | bytes accessed | tf_op | source)
XLA Modules:
  0.0 48.4 jit_solution(7514032383660143037)
XLA Ops:
  0.0 0.0 copy-start
  0.0 1.6 %copy-done = bf16[16,256,256]{2,1,0:T(8,128)(2,1)S(1)} copy-done((bf16[16,256,256]{2,1,0:T(8,128)(2,1)S(1)}, bf16[16,256,256]{2,1,0:T(8,128)(2,1)}, u32[]{:S(2)}) %copy-start) | copy-done | bytes 2097176
  1.6 0.0 copy-start.1
  1.6 1.2 %copy-done.1 = bf16[8,256,256]{2,1,0:T(8,128)(2,1)S(1)} copy-done((bf16[8,256,256]{2,1,0:T(8,128)(2,1)S(1)}, bf16[8,256,256]{2,1,0:T(8,128)(2,1)}, u32[]{:S(2)}) %copy-start.1) | copy-done | bytes 1048600
  2.8 0.0 copy-start.2
  2.8 0.9 %copy-done.2 = bf16[256,256]{1,0:T(8,128)(2,1)S(1)} copy-done((bf16[256,256]{1,0:T(8,128)(2,1)S(1)}, bf16[256,256]{1,0:T(8,128)(2,1)}, u32[]{:S(2)}) %copy-start.2) | copy-done | bytes 131096
  3.7 0.0 copy-start.3
  3.7 0.9 %copy-done.3 = bf16[256,256]{1,0:T(8,128)(2,1)S(1)} copy-done((bf16[256,256]{1,0:T(8,128)(2,1)S(1)}, bf16[256,256]{1,0:T(8,128)(2,1)}, u32[]{:S(2)}) %copy-start.3) | copy-done | bytes 131096
  4.6 0.0 copy-start.4
  4.6 0.7 %copy-done.4 = s32[1,16,384]{2,1,0:T(8,128)S(1)} copy-done((s32[1,16,384]{2,1,0:T(8,128)S(1)}, s32[1,16,384]{2,1,0:T(8,128)}, u32[]{:S(2)}) %copy-start.4) | copy-done | bytes 24600
  5.4 0.0 copy-start.5
  5.4 0.7 %copy-done.5 = s32[1,16,384]{2,1,0:T(8,128)S(1)} copy-done((s32[1,16,384]{2,1,0:T(8,128)S(1)}, s32[1,16,384]{2,1,0:T(8,128)}, u32[]{:S(2)}) %copy-start.5) | copy-done | bytes 24600
  6.1 0.0 copy-start.6
  6.1 0.7 %copy-done.6 = bf16[32,256]{1,0:T(8,128)(2,1)S(1)} copy-done((bf16[32,256]{1,0:T(8,128)(2,1)S(1)}, bf16[32,256]{1,0:T(8,128)(2,1)}, u32[]{:S(2)}) %copy-start.6) | copy-done | bytes 16408
  6.8 0.0 copy-start.7
  6.8 0.7 %copy-done.7 = s32[1,16,24]{2,1,0:T(8,128)S(1)} copy-done((s32[1,16,24]{2,1,0:T(8,128)S(1)}, s32[1,16,24]{2,1,0:T(8,128)}, u32[]{:S(2)}) %copy-start.7) | copy-done | bytes 1560
  7.5 0.0 copy-start.8
  7.5 0.7 %copy-done.8 = s32[1,16,24]{2,1,0:T(8,128)S(1)} copy-done((s32[1,16,24]{2,1,0:T(8,128)S(1)}, s32[1,16,24]{2,1,0:T(8,128)}, u32[]{:S(2)}) %copy-start.8) | copy-done | bytes 1560
  8.2 0.0 copy-start.9
  8.2 0.7 %copy-done.9 = s32[1,16,96]{2,1,0:T(8,128)S(1)} copy-done((s32[1,16,96]{2,1,0:T(8,128)S(1)}, s32[1,16,96]{2,1,0:T(8,128)}, u32[]{:S(2)}) %copy-start.9) | copy-done | bytes 6168
  8.9 0.0 copy-start.10
  8.9 0.7 %copy-done.10 = s32[1,16,96]{2,1,0:T(8,128)S(1)} copy-done((s32[1,16,96]{2,1,0:T(8,128)S(1)}, s32[1,16,96]{2,1,0:T(8,128)}, u32[]{:S(2)}) %copy-start.10) | copy-done | bytes 6168
  9.6 38.1 %shard_map.109 = f32[256,256]{1,0:T(8,128)S(1)} custom-call(bf16[256,256]{1,0:T(8,128)(2,1)S(1)} %copy-done.2, bf16[32,256]{1,0:T(8,128)(2,1)S(1)} %copy-done.6, bf16[256,256]{1,0:T(8,128)(2,1)S(1)} %copy-done.3, bf16[16,256,256]{2,1,0:T(8,128)(2,1)S(1)} %copy-done, bf16[8,256,256]{2,1,0:T(8,128)(2,1)S(1)} %copy-done.1, s32[1,16,24]{2,1,0:T(8,128)S(1)} %copy-done.7, ...), custom_call_target="tpu_custom_call" | custom-call | tf_op jit(solution)/shard_map/pallas_call | solution.py:342
  47.7 0.7 %copy.13 = f32[256,256]{1,0:T(8,128)} copy(f32[256,256]{1,0:T(8,128)S(1)} %shard_map.109) | data formatting | bytes 524288
Async XLA Ops:
  0.0 1.6 %copy-start = (bf16[16,256,256]{2,1,0:T(8,128)(2,1)S(1)}, bf16[16,256,256]{2,1,0:T(8,128)(2,1)}, u32[]{:S(2)}) copy-start(bf16[16,256,256]{2,1,0:T(8,128)(2,1)} %m2l_ref.1) | copy-start | bytes 6291460
  1.6 1.2 %copy-start.1 = (bf16[8,256,256]{2,1,0:T(8,128)(2,1)S(1)}, bf16[8,256,256]{2,1,0:T(8,128)(2,1)}, u32[]{:S(2)}) copy-start(bf16[8,256,256]{2,1,0:T(8,128)(2,1)} %l2l_ref.1) | copy-start | bytes 3145732
  2.8 0.9 %copy-start.2 = (bf16[256,256]{1,0:T(8,128)(2,1)S(1)}, bf16[256,256]{1,0:T(8,128)(2,1)}, u32[]{:S(2)}) copy-start(bf16[256,256]{1,0:T(8,128)(2,1)} %top_ref.1) | copy-start | bytes 393220
  3.7 0.9 %copy-start.3 = (bf16[256,256]{1,0:T(8,128)(2,1)S(1)}, bf16[256,256]{1,0:T(8,128)(2,1)}, u32[]{:S(2)}) copy-start(bf16[256,256]{1,0:T(8,128)(2,1)} %fine_ref.1) | copy-start | bytes 393220
  4.6 0.7 %copy-start.4 = (s32[1,16,384]{2,1,0:T(8,128)S(1)}, s32[1,16,384]{2,1,0:T(8,128)}, u32[]{:S(2)}) copy-start(s32[1,16,384]{2,1,0:T(8,128)} %fsrc_ref.1) | copy-start | bytes 73732
  5.4 0.7 %copy-start.5 = (s32[1,16,384]{2,1,0:T(8,128)S(1)}, s32[1,16,384]{2,1,0:T(8,128)}, u32[]{:S(2)}) copy-start(s32[1,16,384]{2,1,0:T(8,128)} %ftgt_ref.1) | copy-start | bytes 73732
  6.1 0.7 %copy-start.6 = (bf16[32,256]{1,0:T(8,128)(2,1)S(1)}, bf16[32,256]{1,0:T(8,128)(2,1)}, u32[]{:S(2)}) copy-start(bf16[32,256]{1,0:T(8,128)(2,1)} %coarse_ref.1) | copy-start | bytes 49156
  6.8 0.7 %copy-start.7 = (s32[1,16,24]{2,1,0:T(8,128)S(1)}, s32[1,16,24]{2,1,0:T(8,128)}, u32[]{:S(2)}) copy-start(s32[1,16,24]{2,1,0:T(8,128)} %tsrc_ref.1) | copy-start | bytes 4612
  7.5 0.7 %copy-start.8 = (s32[1,16,24]{2,1,0:T(8,128)S(1)}, s32[1,16,24]{2,1,0:T(8,128)}, u32[]{:S(2)}) copy-start(s32[1,16,24]{2,1,0:T(8,128)} %ttgt_ref.1) | copy-start | bytes 4612
  8.2 0.7 %copy-start.9 = (s32[1,16,96]{2,1,0:T(8,128)S(1)}, s32[1,16,96]{2,1,0:T(8,128)}, u32[]{:S(2)}) copy-start(s32[1,16,96]{2,1,0:T(8,128)} %csrc_ref.1) | copy-start | bytes 18436
  8.9 0.7 %copy-start.10 = (s32[1,16,96]{2,1,0:T(8,128)S(1)}, s32[1,16,96]{2,1,0:T(8,128)}, u32[]{:S(2)}) copy-start(s32[1,16,96]{2,1,0:T(8,128)} %ctgt_ref.1) | copy-start | bytes 18436

commit v2 on v1

--- a/solution.py
+++ b/solution.py
@@ -199,8 +199,8 @@
         ccoarse[pl.ds(pl.multiple_of(r * cb, cb), cb)] = dot_nt(targets, sources).astype(BF)
         return 0
 
-    lax.fori_loop(0, classes, coarse_counts, 0)
-    lax.fori_loop(0, classes // 2, fine_counts, 0)
+    lax.fori_loop(0, classes, coarse_counts, 0, unroll=True)
+    lax.fori_loop(0, classes // 2, fine_counts, 0, unroll=True)
 
     for copy in posts:
         copy.wait_recv()
@@ -218,23 +218,19 @@
         ctop[pl.ds(pl.multiple_of(r * quarter, quarter), quarter)] = dot_nt(targets, sources).astype(BF)
         return 0
 
-    lax.fori_loop(0, classes, top_counts, 0)
+    lax.fori_loop(0, classes, top_counts, 0, unroll=True)
 
     def class_columns(r):
-        return pl.ds(pl.multiple_of(r * coeffs, coeffs), coeffs)
+        return pl.ds(r * coeffs, coeffs)
 
     moves[6].wait()
     windows[0].wait_recv()
     windows[1].wait_recv()
 
-    def top_rows(r, _):
-        counts = ctop[pl.ds(pl.multiple_of(r * quarter, quarter), quarter)]
-        hi, lo = split(dot(counts, twin[...]))
-        atop[pl.ds(0, quarter), class_columns(r)] = hi
-        atop[pl.ds(quarter, quarter), class_columns(r)] = lo
-        return 0
-
-    lax.fori_loop(0, classes, top_rows, 0)
+    hi, lo = split(dot(ctop[...], twin[...]))
+    for r in range(classes):
+        atop[pl.ds(0, quarter), class_columns(r)] = hi[r * quarter : (r + 1) * quarter]
+        atop[pl.ds(quarter, quarter), class_columns(r)] = lo[r * quarter : (r + 1) * quarter]
     moves[8].wait()
     part = dot(atop[...], ops[...].reshape(classes * coeffs, coeffs))
     part = part[:quarter] + part[quarter:]
@@ -255,19 +251,16 @@
         copy.start()
     inbox[0] = outbox[j]
 
-    lax.fori_loop(classes // 2, classes, fine_counts, 0)
+    lax.fori_loop(classes // 2, classes, fine_counts, 0, unroll=True)
 
     for copy in windows[2:4]:
         copy.wait_recv()
     moves[7].wait()
 
-    def coarse_rows(r, _):
-        hi, lo = split(dot(ccoarse[pl.ds(pl.multiple_of(r * cb, cb), cb)], cwin[...]))
-        acoarse[pl.ds(0, cb), class_columns(r)] = hi
-        acoarse[pl.ds(cb, cb), class_columns(r)] = lo
-        return 0
-
-    lax.fori_loop(0, classes, coarse_rows, 0)
+    hi, lo = split(dot(ccoarse[...], cwin[...]))
+    for r in range(classes):
+        acoarse[pl.ds(0, cb), class_columns(r)] = hi[r * cb : (r + 1) * cb]
+        acoarse[pl.ds(cb, cb), class_columns(r)] = lo[r * cb : (r + 1) * cb]
     middle = dot(acoarse[...], ops[...].reshape(classes * coeffs, coeffs))
     middle = middle[:cb] + middle[cb:]
 
@@ -280,7 +273,7 @@
         acc[...] += dot(dot(cfine[r], fwin[...]).astype(BF), ops[r])
         return 0
 
-    lax.fori_loop(0, classes, fine_rows, 0)
+    lax.fori_loop(0, classes, fine_rows, 0, unroll=True)
 
     moves[10].wait()
     for copy in shares:
@@ -342,11 +335,11 @@
         return pl.pallas_call(
             functools.partial(kernel, n_row, n_col),
             out_shape=jax.ShapeDtypeStruct((b, coeffs), F32),
-            in_specs=[pl.BlockSpec(memory_space=pl.ANY)] * len(args),
+            in_specs=[pl.BlockSpec(memory_space=pltpu.HBM)] * len(args),
             out_specs=pl.BlockSpec(memory_space=pltpu.VMEM),
             scratch_shapes=scratch,
             compiler_params=pltpu.CompilerParams(
-                collective_id=0, has_side_effects=True, vmem_limit_bytes=40 * 1024 * 1024
+                collective_id=0, has_side_effects=True, vmem_limit_bytes=56 * 1024 * 1024
             ),
         )(*args)
 

time: 49 us -> 31.3 us (0.64)
  the two profiles are of different devices: /device:TPU:5 before, /device:TPU:7 now
where the time goes in v2:
time: 31.3 us; the launch traced here: 31.2 us
  Pallas kernels  29.5 us (94%)
  local copies, waits for them, and re-layouts  1.67 us (5%)
    pallas_call x1, Pallas kernels, per_device(): pl.pallas_call(functools.partial(kernel, n_row, n_col), out_shape=jax.Sha...  29.5 us
    unnamed x1, local copies, waits for them, and re-layouts  1.67 us

profile of v2, /device:TPU:7, one launch (start us, length us, event | category | flops | bytes accessed | tf_op | source)
XLA Modules:
  0.0 31.2 jit_solution(7798399494586776576)
XLA Ops:
  0.0 29.5 %shard_map.109 = f32[256,256]{1,0:T(8,128)} custom-call(bf16[256,256]{1,0:T(8,128)(2,1)} %top_ref.1, bf16[32,256]{1,0:T(8,128)(2,1)} %coarse_ref.1, bf16[256,256]{1,0:T(8,128)(2,1)} %fine_ref.1, bf16[16,256,256]{2,1,0:T(8,128)(2,1)} %m2l_ref.1, bf16[8,256,256]{2,1,0:T(8,128)(2,1)} %l2l_ref.1, s32[1,16,24]{2,1,0:T(8,128)} %tsrc_ref.1, s32[1,16,24]{2,1,0:T(8,128)} %ttgt_ref.1, ...), custom_call_target="tpu_custom_call" | custom-call | tf_op jit(solution)/shard_map/pallas_call | solution.py:335
  29.5 1.7 %copy.13 = f32[256,256]{1,0:T(8,128)} copy(f32[256,256]{1,0:T(8,128)} %shard_map.109) | data formatting | bytes 524288

commit v3 on v2

--- a/solution.py
+++ b/solution.py
@@ -9,6 +9,8 @@
 
 CORES = 2
 XS = 4
+EARLY = 12
+MIDDLE = 16
 MESH = pl.DeviceIdType.MESH
 BF = jnp.bfloat16
 F32 = jnp.float32
@@ -121,11 +123,20 @@
         return (row, x * planes + lax.rem(j + k, planes))
 
     barrier = pltpu.get_barrier_semaphore()
-    partners = [after, before, above, below]
-    partners += [mate(k) for k in range(1, mates)]
+    partners = [mate(k) for k in range(1, mates)]
     partners += [peer(k) for k in range(1, planes)]
     for partner in partners:
         pl.semaphore_signal(barrier, inc=1, device_id=partner, device_id_type=MESH)
+    has_above, has_below = row < n_row - 1, row > 0
+    has_after, has_before = device < total - 1, device > 0
+    expected = len(partners)
+    edges = [(has_above, above), (has_below, below), (has_after, after), (has_before, before)]
+    for there, partner in edges:
+        expected += jnp.where(there, 1, 0)
+
+        @pl.when(there)
+        def _(partner=partner):
+            pl.semaphore_signal(barrier, inc=1, device_id=partner, device_id_type=MESH)
 
     own_top = top_ref.at[pl.ds(pl.multiple_of(core * half, half), half)]
     moves = [
@@ -156,38 +167,60 @@
     mine[...] = columns
     lists[pl.ds(0, capt)] = columns
 
-    pl.semaphore_wait(barrier, len(partners))
-
-    def remote(src, dst, send, recv, to):
-        return pltpu.make_async_remote_copy(
-            src_ref=src, dst_ref=dst, send_sem=send, recv_sem=recv, device_id=to, device_id_type=MESH
-        )
-
-    windows = [
-        (own_top, twin.at[pl.ds(0, half)], above),
-        (own_top, twin.at[pl.ds(2 * half, half)], below),
-        (coarse_ref, cwin.at[pl.ds(0, cb)], after),
-        (coarse_ref, cwin.at[pl.ds(2 * cb, cb)], before),
-        (fine_ref, fwin.at[pl.ds(0, b)], after),
-        (fine_ref, fwin.at[pl.ds(2 * b, b)], before),
-    ]
-    windows = [remote(s, d, wsend.at[i], wrecv.at[i], to) for i, (s, d, to) in enumerate(windows)]
-    posts = [
-        remote(mine, lists.at[pl.ds(k * capt, capt)], lsend.at[k], lrecv.at[k], mate(k))
-        for k in range(1, mates)
-    ]
-    for copy in windows[:2] + posts + windows[2:]:
-        copy.start()
-
-    for i in (2, 3, 4, 5):
-        moves[i].wait()
-
     def fine_counts(r, _):
         targets = onehot(b, ftgt[0, pl.ds(r, 1), :])
         sources = onehot(3 * b, fsrc[0, pl.ds(r, 1), :])
         cfine[r] = dot_nt(targets, sources).astype(BF)
         return 0
 
+    moves[2].wait()
+    moves[3].wait()
+    lax.fori_loop(0, EARLY, fine_counts, 0, unroll=True)
+
+    pl.semaphore_wait(barrier, expected)
+
+    def remote(src, dst, send, recv, to):
+        return pltpu.make_async_remote_copy(
+            src_ref=src, dst_ref=dst, send_sem=send, recv_sem=recv, device_id=to, device_id_type=MESH
+        )
+
+    windows = [
+        (own_top, twin.at[pl.ds(0, half)], above, has_above, has_below),
+        (own_top, twin.at[pl.ds(2 * half, half)], below, has_below, has_above),
+        (coarse_ref, cwin.at[pl.ds(0, cb)], after, has_after, has_before),
+        (coarse_ref, cwin.at[pl.ds(2 * cb, cb)], before, has_before, has_after),
+        (fine_ref, fwin.at[pl.ds(0, b)], after, has_after, has_before),
+        (fine_ref, fwin.at[pl.ds(2 * b, b)], before, has_before, has_after),
+    ]
+    windows = [
+        (remote(s, d, wsend.at[i], wrecv.at[i], to), d, sent, received)
+        for i, (s, d, to, sent, received) in enumerate(windows)
+    ]
+
+    def start(window):
+        pl.when(window[2])(window[0].start)
+
+    def receive(window):
+        pl.when(window[3])(window[0].wait_recv)
+
+    posts = [
+        remote(mine, lists.at[pl.ds(k * capt, capt)], lsend.at[k], lrecv.at[k], mate(k))
+        for k in range(1, mates)
+    ]
+    for window in windows[:2]:
+        start(window)
+    for copy in posts:
+        copy.start()
+    for window in windows[2:]:
+        start(window)
+    for _, there, _, received in windows:
+
+        @pl.when(jnp.logical_not(received))
+        def _(there=there):
+            there[...] = jnp.zeros(there.shape, BF)
+
+    moves[4].wait()
+    moves[5].wait()
     cpick[...] = jnp.full(cpick.shape, -1, jnp.int32)
     cpick[pl.ds(0, classes), pl.ds(0, capc)] = csrc[0] - (device - 1) * cb
     cpick[pl.ds(classes, classes), pl.ds(0, capc)] = ctgt[0]
@@ -200,7 +233,7 @@
         return 0
 
     lax.fori_loop(0, classes, coarse_counts, 0, unroll=True)
-    lax.fori_loop(0, classes // 2, fine_counts, 0, unroll=True)
+    lax.fori_loop(EARLY, MIDDLE, fine_counts, 0, unroll=True)
 
     for copy in posts:
         copy.wait_recv()
@@ -224,8 +257,8 @@
         return pl.ds(r * coeffs, coeffs)
 
     moves[6].wait()
-    windows[0].wait_recv()
-    windows[1].wait_recv()
+    receive(windows[0])
+    receive(windows[1])
 
     hi, lo = split(dot(ctop[...], twin[...]))
     for r in range(classes):
@@ -251,10 +284,10 @@
         copy.start()
     inbox[0] = outbox[j]
 
-    lax.fori_loop(classes // 2, classes, fine_counts, 0, unroll=True)
-
-    for copy in windows[2:4]:
-        copy.wait_recv()
+    lax.fori_loop(MIDDLE, classes, fine_counts, 0, unroll=True)
+
+    for window in windows[2:4]:
+        receive(window)
     moves[7].wait()
 
     hi, lo = split(dot(ccoarse[...], cwin[...]))
@@ -264,8 +297,8 @@
     middle = dot(acoarse[...], ops[...].reshape(classes * coeffs, coeffs))
     middle = middle[:cb] + middle[cb:]
 
-    for copy in windows[4:]:
-        copy.wait_recv()
+    for window in windows[4:]:
+        receive(window)
     moves[9].wait()
     acc[...] = jnp.zeros_like(acc)
 
@@ -286,7 +319,9 @@
     coarse = coarse.astype(BF).astype(F32)
     out_ref[...] = children(coarse, l2l[...]) + acc[...]
 
-    for copy in windows + posts + shares:
+    for window in windows:
+        pl.when(window[2])(window[0].wait_send)
+    for copy in posts + shares:
         copy.wait_send()
 
 

time: 31.3 us -> 25.4 us (0.81)
  the two profiles are of different devices: /device:TPU:7 before, /device:TPU:1 now
where the time goes in v3:
time: 25.4 us; the launch traced here: 25.2 us
  Pallas kernels  23.5 us (93%)
  local copies, waits for them, and re-layouts  1.67 us (7%)
    pallas_call x1, Pallas kernels, per_device(): pl.pallas_call(functools.partial(kernel, n_row, n_col), out_shape=jax.Sha...  23.5 us
    unnamed x1, local copies, waits for them, and re-layouts  1.67 us

profile of v3, /device:TPU:1, one launch (start us, length us, event | category | flops | bytes accessed | tf_op | source)
XLA Modules:
  0.0 25.2 jit_solution(7723006422351716262)
XLA Ops:
  0.0 23.5 %shard_map.109 = f32[256,256]{1,0:T(8,128)} custom-call(bf16[256,256]{1,0:T(8,128)(2,1)} %top_ref.1, bf16[32,256]{1,0:T(8,128)(2,1)} %coarse_ref.1, bf16[256,256]{1,0:T(8,128)(2,1)} %fine_ref.1, bf16[16,256,256]{2,1,0:T(8,128)(2,1)} %m2l_ref.1, bf16[8,256,256]{2,1,0:T(8,128)(2,1)} %l2l_ref.1, s32[1,16,24]{2,1,0:T(8,128)} %tsrc_ref.1, s32[1,16,24]{2,1,0:T(8,128)} %ttgt_ref.1, ...), custom_call_target="tpu_custom_call" | custom-call | tf_op jit(solution)/shard_map/pallas_call | solution.py:370
  23.5 1.7 %copy.13 = f32[256,256]{1,0:T(8,128)} copy(f32[256,256]{1,0:T(8,128)} %shard_map.109) | data formatting | bytes 524288

commit v4 on v3

--- a/solution.py
+++ b/solution.py
@@ -122,22 +122,6 @@
     def peer(k):
         return (row, x * planes + lax.rem(j + k, planes))
 
-    barrier = pltpu.get_barrier_semaphore()
-    partners = [mate(k) for k in range(1, mates)]
-    partners += [peer(k) for k in range(1, planes)]
-    for partner in partners:
-        pl.semaphore_signal(barrier, inc=1, device_id=partner, device_id_type=MESH)
-    has_above, has_below = row < n_row - 1, row > 0
-    has_after, has_before = device < total - 1, device > 0
-    expected = len(partners)
-    edges = [(has_above, above), (has_below, below), (has_after, after), (has_before, before)]
-    for there, partner in edges:
-        expected += jnp.where(there, 1, 0)
-
-        @pl.when(there)
-        def _(partner=partner):
-            pl.semaphore_signal(barrier, inc=1, device_id=partner, device_id_type=MESH)
-
     own_top = top_ref.at[pl.ds(pl.multiple_of(core * half, half), half)]
     moves = [
         (tsrc_ref, tsrc),
@@ -153,7 +137,27 @@
         (l2l_ref, l2l),
     ]
     moves = [pltpu.make_async_copy(s, d, local_sem.at[i]) for i, (s, d) in enumerate(moves)]
-    for move in moves:
+    for move in moves[:4]:
+        move.start()
+
+    barrier = pltpu.get_barrier_semaphore()
+    mate_order = sorted(range(1, mates), key=lambda k: -min(k, mates - k))
+    peer_order = sorted(range(1, planes), key=lambda k: -min(k, planes - k))
+    partners = [peer(k) for k in peer_order] + [mate(k) for k in mate_order]
+    for partner in partners:
+        pl.semaphore_signal(barrier, inc=1, device_id=partner, device_id_type=MESH)
+    has_above, has_below = row < n_row - 1, row > 0
+    has_after, has_before = device < total - 1, device > 0
+    expected = len(partners)
+    edges = [(has_above, above), (has_below, below), (has_after, after), (has_before, before)]
+    for there, partner in edges:
+        expected += jnp.where(there, 1, 0)
+
+        @pl.when(there)
+        def _(partner=partner):
+            pl.semaphore_signal(barrier, inc=1, device_id=partner, device_id_type=MESH)
+
+    for move in moves[4:]:
         move.start()
 
     square[...] = jnp.zeros_like(square)
@@ -204,14 +208,14 @@
         pl.when(window[3])(window[0].wait_recv)
 
     posts = [
-        remote(mine, lists.at[pl.ds(k * capt, capt)], lsend.at[k], lrecv.at[k], mate(k))
-        for k in range(1, mates)
-    ]
-    for window in windows[:2]:
-        start(window)
+        remote(mine, lists.at[pl.ds(k * capt, capt)], lsend, lrecv, mate(k))
+        for k in mate_order
+    ]
+    arrived = pl.ds(capt, (mates - 1) * capt)
+    all_posts = remote(lists.at[arrived], lists.at[arrived], lsend, lrecv, mate(1))
     for copy in posts:
         copy.start()
-    for window in windows[2:]:
+    for window in windows:
         start(window)
     for _, there, _, received in windows:
 
@@ -235,8 +239,7 @@
     lax.fori_loop(0, classes, coarse_counts, 0, unroll=True)
     lax.fori_loop(EARLY, MIDDLE, fine_counts, 0, unroll=True)
 
-    for copy in posts:
-        copy.wait_recv()
+    all_posts.wait_recv()
     rows = lists[...].T[: 2 * classes]
     offset = rows[:classes] - (row - 1) * seg
     which = jnp.where(offset >= seg, 1, 0) + jnp.where(offset >= 2 * seg, 1, 0)
@@ -277,9 +280,11 @@
         outbox[2 * i] = even[i]
         outbox[2 * i + 1] = odd[i]
     shares = [
-        remote(outbox.at[lax.rem(j + k, planes)], inbox.at[k], rsend.at[k], rrecv.at[k], peer(k))
-        for k in range(1, planes)
-    ]
+        remote(outbox.at[lax.rem(j + k, planes)], inbox.at[k], rsend, rrecv, peer(k))
+        for k in peer_order
+    ]
+    arrived = pl.ds(1, planes - 1)
+    all_shares = remote(outbox.at[arrived], inbox.at[arrived], rsend, rrecv, peer(1))
     for copy in shares:
         copy.start()
     inbox[0] = outbox[j]
@@ -309,8 +314,11 @@
     lax.fori_loop(0, classes, fine_rows, 0, unroll=True)
 
     moves[10].wait()
-    for copy in shares:
-        copy.wait_recv()
+    for window in windows:
+        pl.when(window[2])(window[0].wait_send)
+    all_posts.wait_send()
+    all_shares.wait_send()
+    all_shares.wait_recv()
     summed = inbox[0]
     for k in range(1, planes):
         summed += inbox[k]
@@ -318,11 +326,6 @@
     coarse = children(top, l2l[...]) + middle
     coarse = coarse.astype(BF).astype(F32)
     out_ref[...] = children(coarse, l2l[...]) + acc[...]
-
-    for window in windows:
-        pl.when(window[2])(window[0].wait_send)
-    for copy in posts + shares:
-        copy.wait_send()
 
 
 def solution(mesh):
@@ -362,10 +365,10 @@
             pltpu.SemaphoreType.DMA((11,)),
             pltpu.SemaphoreType.DMA((6,)),
             pltpu.SemaphoreType.DMA((6,)),
-            pltpu.SemaphoreType.DMA((mates,)),
-            pltpu.SemaphoreType.DMA((mates,)),
-            pltpu.SemaphoreType.DMA((planes,)),
-            pltpu.SemaphoreType.DMA((planes,)),
+            pltpu.SemaphoreType.DMA,
+            pltpu.SemaphoreType.DMA,
+            pltpu.SemaphoreType.DMA,
+            pltpu.SemaphoreType.DMA,
         ]
         return pl.pallas_call(
             functools.partial(kernel, n_row, n_col),
@@ -374,9 +377,9 @@
             out_specs=pl.BlockSpec(memory_space=pltpu.VMEM),
             scratch_shapes=scratch,
             compiler_params=pltpu.CompilerParams(
-                collective_id=0, has_side_effects=True, vmem_limit_bytes=56 * 1024 * 1024
+                collective_id=0, has_side_effects=True, vmem_limit_bytes=40 * 1024 * 1024
             ),
-        )(*args)
+        )(*[pltpu.with_memory_space_constraint(a, pltpu.HBM) for a in args])
 
     both = P(("row", "col"), None)
     lists = P(("row", "col"), None, None)

time: 25.4 us -> 22.5 us (0.89)
  Pallas kernels: 23.5 us -> 21.6 us
  local copies, waits for them, and re-layouts: 1.67 us -> 0.71 us
    pallas_call x1, Pallas kernels: 23.5 us -> 21.6 us  [per_device(): pl.pallas_call(functools.partial(kernel, n_row, n_col), out_shape=jax.Sha...]
    unnamed x1, local copies, waits for them, and re-layouts: 1.67 us -> 0.71 us
where the time goes in v4:
time: 22.5 us; the launch traced here: 22.3 us
  Pallas kernels  21.6 us (96%)
  local copies, waits for them, and re-layouts  0.71 us (3%)
    pallas_call x1, Pallas kernels, per_device(): pl.pallas_call(functools.partial(kernel, n_row, n_col), out_shape=jax.Sha...  21.6 us
    unnamed x1, local copies, waits for them, and re-layouts  0.71 us

profile of v4, /device:TPU:1, one launch (start us, length us, event | category | flops | bytes accessed | tf_op | source)
XLA Modules:
  0.0 22.3 jit_solution(9233221178159732807)
XLA Ops:
  0.0 21.6 %shard_map.109 = f32[256,256]{1,0:T(8,128)S(1)} custom-call(bf16[256,256]{1,0:T(8,128)(2,1)} %top_ref.1, bf16[32,256]{1,0:T(8,128)(2,1)} %coarse_ref.1, bf16[256,256]{1,0:T(8,128)(2,1)} %fine_ref.1, bf16[16,256,256]{2,1,0:T(8,128)(2,1)} %m2l_ref.1, bf16[8,256,256]{2,1,0:T(8,128)(2,1)} %l2l_ref.1, s32[1,16,24]{2,1,0:T(8,128)} %tsrc_ref.1, ...), custom_call_target="tpu_custom_call" | custom-call | tf_op jit(solution)/shard_map/pallas_call | solution.py:373
  21.6 0.7 %copy.13 = f32[256,256]{1,0:T(8,128)} copy(f32[256,256]{1,0:T(8,128)S(1)} %shard_map.109) | data formatting | bytes 524288

commit v5 on v4

--- a/solution.py
+++ b/solution.py
@@ -11,14 +11,16 @@
 XS = 4
 EARLY = 12
 MIDDLE = 16
+TOGETHER = 4
 MESH = pl.DeviceIdType.MESH
 BF = jnp.bfloat16
 F32 = jnp.float32
+F8 = jnp.float8_e4m3fn
 
 
 def onehot(rows, picks):
     number = lax.broadcasted_iota(jnp.int32, (rows, picks.shape[1]), 0)
-    return jnp.where(number == picks, 1.0, 0.0).astype(BF)
+    return jnp.where(number == picks, 1.0, 0.0).astype(F8)
 
 
 def dot(a, b):
@@ -74,7 +76,6 @@
     lists,
     tpick,
     cpick,
-    ctop,
     ccoarse,
     cfine,
     atop,
@@ -89,6 +90,7 @@
     lrecv,
     rsend,
     rrecv,
+    learnt,
 ):
     classes, coeffs = m2l_ref.shape[0], m2l_ref.shape[1]
     seg = top_ref.shape[0]
@@ -143,7 +145,8 @@
     barrier = pltpu.get_barrier_semaphore()
     mate_order = sorted(range(1, mates), key=lambda k: -min(k, mates - k))
     peer_order = sorted(range(1, planes), key=lambda k: -min(k, planes - k))
-    partners = [peer(k) for k in peer_order] + [mate(k) for k in mate_order]
+    near = [1, 2, planes - 2, planes - 1]
+    partners = [mate(k) for k in mate_order] + [peer(k) for k in near]
     for partner in partners:
         pl.semaphore_signal(barrier, inc=1, device_id=partner, device_id_type=MESH)
     has_above, has_below = row < n_row - 1, row > 0
@@ -217,6 +220,8 @@
         copy.start()
     for window in windows:
         start(window)
+    for k in (2, planes - 2):
+        pl.semaphore_signal(learnt.at[0], inc=1, device_id=peer(k), device_id_type=MESH)
     for _, there, _, received in windows:
 
         @pl.when(jnp.logical_not(received))
@@ -237,6 +242,9 @@
         return 0
 
     lax.fori_loop(0, classes, coarse_counts, 0, unroll=True)
+    pl.semaphore_wait(learnt.at[0], 2)
+    for k in (4, planes - 4):
+        pl.semaphore_signal(learnt.at[1], inc=1, device_id=peer(k), device_id_type=MESH)
     lax.fori_loop(EARLY, MIDDLE, fine_counts, 0, unroll=True)
 
     all_posts.wait_recv()
@@ -248,26 +256,26 @@
     tpick[pl.ds(0, classes)] = inside
     tpick[pl.ds(classes, classes)] = rows[classes:] - x * quarter
 
-    def top_counts(r, _):
-        targets = onehot(quarter, tpick[pl.ds(classes + r, 1), :])
-        sources = onehot(3 * half, tpick[pl.ds(r, 1), :])
-        ctop[pl.ds(pl.multiple_of(r * quarter, quarter), quarter)] = dot_nt(targets, sources).astype(BF)
-        return 0
-
-    lax.fori_loop(0, classes, top_counts, 0, unroll=True)
-
     def class_columns(r):
         return pl.ds(r * coeffs, coeffs)
 
     moves[6].wait()
     receive(windows[0])
     receive(windows[1])
-
-    hi, lo = split(dot(ctop[...], twin[...]))
-    for r in range(classes):
-        atop[pl.ds(0, quarter), class_columns(r)] = hi[r * quarter : (r + 1) * quarter]
-        atop[pl.ds(quarter, quarter), class_columns(r)] = lo[r * quarter : (r + 1) * quarter]
     moves[8].wait()
+
+    def top_counts(r):
+        targets = onehot(quarter, tpick[pl.ds(classes + r, 1), :])
+        sources = onehot(3 * half, tpick[pl.ds(r, 1), :])
+        return dot_nt(targets, sources).astype(BF)
+
+    for first in range(0, classes, TOGETHER):
+        group = range(first, first + TOGETHER)
+        counts = jnp.concatenate([top_counts(r) for r in group], axis=0)
+        hi, lo = split(dot(counts, twin[...]))
+        for i, r in enumerate(group):
+            atop[pl.ds(0, quarter), class_columns(r)] = hi[i * quarter : (i + 1) * quarter]
+            atop[pl.ds(quarter, quarter), class_columns(r)] = lo[i * quarter : (i + 1) * quarter]
     part = dot(atop[...], ops[...].reshape(classes * coeffs, coeffs))
     part = part[:quarter] + part[quarter:]
     lanes = coeffs // 2
@@ -285,6 +293,7 @@
     ]
     arrived = pl.ds(1, planes - 1)
     all_shares = remote(outbox.at[arrived], inbox.at[arrived], rsend, rrecv, peer(1))
+    pl.semaphore_wait(learnt.at[1], 2)
     for copy in shares:
         copy.start()
     inbox[0] = outbox[j]
@@ -325,7 +334,9 @@
     top = jnp.concatenate([summed[:4], summed[4:]], axis=1).astype(BF).astype(F32)
     coarse = children(top, l2l[...]) + middle
     coarse = coarse.astype(BF).astype(F32)
-    out_ref[...] = children(coarse, l2l[...]) + acc[...]
+    parents = coarse.astype(BF)
+    fine = jnp.stack([dot(parents, l2l[o]) for o in range(l2l.shape[0])], axis=1)
+    out_ref[...] = fine.reshape(b, coeffs) + acc[...]
 
 
 def solution(mesh):
@@ -354,7 +365,6 @@
             pltpu.VMEM((slots, pad), jnp.int32),
             pltpu.VMEM((2 * classes, slots), jnp.int32),
             pltpu.VMEM((2 * classes, pad), jnp.int32),
-            pltpu.VMEM((classes * quarter, 3 * seg // CORES), BF),
             pltpu.VMEM((classes * cb, crows), BF),
             pltpu.VMEM((classes, b, 3 * b), BF),
             pltpu.VMEM((2 * quarter, classes * coeffs), BF),
@@ -369,6 +379,7 @@
             pltpu.SemaphoreType.DMA,
             pltpu.SemaphoreType.DMA,
             pltpu.SemaphoreType.DMA,
+            pltpu.SemaphoreType.REGULAR((2,)),
         ]
         return pl.pallas_call(
             functools.partial(kernel, n_row, n_col),

time: 22.5 us -> 21.7 us (0.964)
  the two profiles are of different devices: /device:TPU:1 before, /device:TPU:192 now
where the time goes in v5:
time: 21.7 us; the launch traced here: 21.2 us
  Pallas kernels  20.5 us (94%)
  local copies, waits for them, and re-layouts  0.71 us (3%)
    pallas_call x1, Pallas kernels, per_device(): pl.pallas_call(functools.partial(kernel, n_row, n_col), out_shape=jax.Sha...  20.5 us
    unnamed x1, local copies, waits for them, and re-layouts  0.71 us

profile of v5, /device:TPU:192, one launch (start us, length us, event | category | flops | bytes accessed | tf_op | source)
XLA Modules:
  0.0 21.2 jit_solution(13051514117162759922)
XLA Ops:
  0.0 20.5 %shard_map.109 = f32[256,256]{1,0:T(8,128)S(1)} custom-call(bf16[256,256]{1,0:T(8,128)(2,1)} %top_ref.1, bf16[32,256]{1,0:T(8,128)(2,1)} %coarse_ref.1, bf16[256,256]{1,0:T(8,128)(2,1)} %fine_ref.1, bf16[16,256,256]{2,1,0:T(8,128)(2,1)} %m2l_ref.1, bf16[8,256,256]{2,1,0:T(8,128)(2,1)} %l2l_ref.1, s32[1,16,24]{2,1,0:T(8,128)} %tsrc_ref.1, ...), custom_call_target="tpu_custom_call" | custom-call | tf_op jit(solution)/shard_map/pallas_call | solution.py:384
  20.5 0.7 %copy.13 = f32[256,256]{1,0:T(8,128)} copy(f32[256,256]{1,0:T(8,128)S(1)} %shard_map.109) | data formatting | bytes 524288

commit v6 on v5

--- a/solution.py
+++ b/solution.py
@@ -9,7 +9,7 @@
 
 CORES = 2
 XS = 4
-EARLY = 12
+EARLY = 6
 MIDDLE = 16
 TOGETHER = 4
 MESH = pl.DeviceIdType.MESH
@@ -164,15 +164,18 @@
         move.start()
 
     square[...] = jnp.zeros_like(square)
-    unused = lists.shape[0] - mates * capt
-    lists[pl.ds(mates * capt, unused)] = jnp.full((unused, lists.shape[1]), -1, jnp.int32)
+    unused = lists.shape[0] - mates * 8
+    lists[pl.ds(mates * 8, unused)] = jnp.full((unused, lists.shape[1]), -1, jnp.int32)
     moves[0].wait()
     moves[1].wait()
     square[pl.ds(0, classes), pl.ds(0, capt)] = tsrc[0]
     square[pl.ds(classes, classes), pl.ds(0, capt)] = ttgt[0]
-    columns = square[...].T[:capt]
-    mine[...] = columns
-    lists[pl.ds(0, capt)] = columns
+    columns = square[...].T
+    packed = columns[:8]
+    for g in range(1, capt // 8):
+        packed += pltpu.roll(columns[8 * g : 8 * g + 8], g * 2 * classes, 1)
+    mine[...] = packed
+    lists[pl.ds(0, 8)] = packed
 
     def fine_counts(r, _):
         targets = onehot(b, ftgt[0, pl.ds(r, 1), :])
@@ -211,10 +214,10 @@
         pl.when(window[3])(window[0].wait_recv)
 
     posts = [
-        remote(mine, lists.at[pl.ds(k * capt, capt)], lsend, lrecv, mate(k))
+        remote(mine, lists.at[pl.ds(k * 8, 8)], lsend, lrecv, mate(k))
         for k in mate_order
     ]
-    arrived = pl.ds(capt, (mates - 1) * capt)
+    arrived = pl.ds(8, (mates - 1) * 8)
     all_posts = remote(lists.at[arrived], lists.at[arrived], lsend, lrecv, mate(1))
     for copy in posts:
         copy.start()
@@ -248,7 +251,11 @@
     lax.fori_loop(EARLY, MIDDLE, fine_counts, 0, unroll=True)
 
     all_posts.wait_recv()
-    rows = lists[...].T[: 2 * classes]
+    turned = lists[...].T
+    blocks = [turned[g * 2 * classes : (g + 1) * 2 * classes] for g in range(capt // 8)]
+    lane = lax.broadcasted_iota(jnp.int32, blocks[0].shape, 1)
+    pair = jnp.where(lane < 8 * mates, blocks[0], pltpu.roll(blocks[1], 8 * mates, 1))
+    rows = jnp.concatenate([pair, blocks[2]], axis=1)
     offset = rows[:classes] - (row - 1) * seg
     which = jnp.where(offset >= seg, 1, 0) + jnp.where(offset >= 2 * seg, 1, 0)
     inside = offset - which * seg - core * half
@@ -361,8 +368,8 @@
             pltpu.VMEM(l2l.shape, BF),
             *[pltpu.VMEM(a.shape, jnp.int32) for a in (tsrc, ttgt, csrc, ctgt, fsrc, ftgt)],
             pltpu.VMEM((pad, pad), jnp.int32),
-            pltpu.VMEM((capt, pad), jnp.int32),
-            pltpu.VMEM((slots, pad), jnp.int32),
+            pltpu.VMEM((8, pad), jnp.int32),
+            pltpu.VMEM((pad, pad), jnp.int32),
             pltpu.VMEM((2 * classes, slots), jnp.int32),
             pltpu.VMEM((2 * classes, pad), jnp.int32),
             pltpu.VMEM((classes * cb, crows), BF),

time: 21.7 us -> 21.3 us (0.982)
  Pallas kernels: 20.5 us -> 20.2 us
    pallas_call x1, Pallas kernels: 20.5 us -> 20.2 us  [per_device(): pl.pallas_call(functools.partial(kernel, n_row, n_col), out_shape=jax.Sha...]
where the time goes in v6:
time: 21.3 us; the launch traced here: 20.9 us
  Pallas kernels  20.2 us (95%)
  local copies, waits for them, and re-layouts  0.71 us (3%)
    pallas_call x1, Pallas kernels, per_device(): pl.pallas_call(functools.partial(kernel, n_row, n_col), out_shape=jax.Sha...  20.2 us
    unnamed x1, local copies, waits for them, and re-layouts  0.71 us

profile of v6, /device:TPU:192, one launch (start us, length us, event | category | flops | bytes accessed | tf_op | source)
XLA Modules:
  0.0 20.9 jit_solution(15064736602451922770)
XLA Ops:
  0.0 20.2 %shard_map.109 = f32[256,256]{1,0:T(8,128)S(1)} custom-call(bf16[256,256]{1,0:T(8,128)(2,1)} %top_ref.1, bf16[32,256]{1,0:T(8,128)(2,1)} %coarse_ref.1, bf16[256,256]{1,0:T(8,128)(2,1)} %fine_ref.1, bf16[16,256,256]{2,1,0:T(8,128)(2,1)} %m2l_ref.1, bf16[8,256,256]{2,1,0:T(8,128)(2,1)} %l2l_ref.1, s32[1,16,24]{2,1,0:T(8,128)} %tsrc_ref.1, ...), custom_call_target="tpu_custom_call" | custom-call | tf_op jit(solution)/shard_map/pallas_call | solution.py:391
  20.2 0.7 %copy.13 = f32[256,256]{1,0:T(8,128)} copy(f32[256,256]{1,0:T(8,128)S(1)} %shard_map.109) | data formatting | bytes 524288

commit v7 on v6

--- a/solution.py
+++ b/solution.py
@@ -221,10 +221,10 @@
     all_posts = remote(lists.at[arrived], lists.at[arrived], lsend, lrecv, mate(1))
     for copy in posts:
         copy.start()
+    for k in (2, planes - 2):
+        pl.semaphore_signal(learnt.at[0], inc=1, device_id=peer(k), device_id_type=MESH)
     for window in windows:
         start(window)
-    for k in (2, planes - 2):
-        pl.semaphore_signal(learnt.at[0], inc=1, device_id=peer(k), device_id_type=MESH)
     for _, there, _, received in windows:
 
         @pl.when(jnp.logical_not(received))
@@ -245,10 +245,10 @@
         return 0
 
     lax.fori_loop(0, classes, coarse_counts, 0, unroll=True)
+    lax.fori_loop(EARLY, MIDDLE, fine_counts, 0, unroll=True)
     pl.semaphore_wait(learnt.at[0], 2)
     for k in (4, planes - 4):
         pl.semaphore_signal(learnt.at[1], inc=1, device_id=peer(k), device_id_type=MESH)
-    lax.fori_loop(EARLY, MIDDLE, fine_counts, 0, unroll=True)
 
     all_posts.wait_recv()
     turned = lists[...].T

time: 21.3 us -> 21.3 us (level)
  no operation moved by 1% of the time
where the time goes in v7:
time: 21.3 us; the launch traced here: 20.9 us
  Pallas kernels  20.2 us (95%)
  local copies, waits for them, and re-layouts  0.71 us (3%)
    pallas_call x1, Pallas kernels, per_device(): pl.pallas_call(functools.partial(kernel, n_row, n_col), out_shape=jax.Sha...  20.2 us
    unnamed x1, local copies, waits for them, and re-layouts  0.71 us

profile of v7, /device:TPU:192, one launch (start us, length us, event | category | flops | bytes accessed | tf_op | source)
XLA Modules:
  0.0 20.9 jit_solution(10140067298915977021)
XLA Ops:
  0.0 20.2 %shard_map.109 = f32[256,256]{1,0:T(8,128)S(1)} custom-call(bf16[256,256]{1,0:T(8,128)(2,1)} %top_ref.1, bf16[32,256]{1,0:T(8,128)(2,1)} %coarse_ref.1, bf16[256,256]{1,0:T(8,128)(2,1)} %fine_ref.1, bf16[16,256,256]{2,1,0:T(8,128)(2,1)} %m2l_ref.1, bf16[8,256,256]{2,1,0:T(8,128)(2,1)} %l2l_ref.1, s32[1,16,24]{2,1,0:T(8,128)} %tsrc_ref.1, ...), custom_call_target="tpu_custom_call" | custom-call | tf_op jit(solution)/shard_map/pallas_call | solution.py:391
  20.2 0.7 %copy.13 = f32[256,256]{1,0:T(8,128)} copy(f32[256,256]{1,0:T(8,128)S(1)} %shard_map.109) | data formatting | bytes 524288

commit v8 on v7

--- a/solution.py
+++ b/solution.py
@@ -9,8 +9,8 @@
 
 CORES = 2
 XS = 4
-EARLY = 6
-MIDDLE = 16
+EARLY = 4
+MIDDLE = 13
 TOGETHER = 4
 MESH = pl.DeviceIdType.MESH
 BF = jnp.bfloat16

time: 21.3 us -> 21.3 us (level)
  no operation moved by 1% of the time
where the time goes in v8:
time: 21.3 us; the launch traced here: 20.9 us
  Pallas kernels  20.2 us (95%)
  local copies, waits for them, and re-layouts  0.71 us (3%)
    pallas_call x1, Pallas kernels, per_device(): pl.pallas_call(functools.partial(kernel, n_row, n_col), out_shape=jax.Sha...  20.2 us
    unnamed x1, local copies, waits for them, and re-layouts  0.71 us

profile of v8, /device:TPU:192, one launch (start us, length us, event | category | flops | bytes accessed | tf_op | source)
XLA Modules:
  0.0 20.9 jit_solution(12794189042200286667)
XLA Ops:
  0.0 20.2 %shard_map.109 = f32[256,256]{1,0:T(8,128)S(1)} custom-call(bf16[256,256]{1,0:T(8,128)(2,1)} %top_ref.1, bf16[32,256]{1,0:T(8,128)(2,1)} %coarse_ref.1, bf16[256,256]{1,0:T(8,128)(2,1)} %fine_ref.1, bf16[16,256,256]{2,1,0:T(8,128)(2,1)} %m2l_ref.1, bf16[8,256,256]{2,1,0:T(8,128)(2,1)} %l2l_ref.1, s32[1,16,24]{2,1,0:T(8,128)} %tsrc_ref.1, ...), custom_call_target="tpu_custom_call" | custom-call | tf_op jit(solution)/shard_map/pallas_call | solution.py:391
  20.2 0.7 %copy.13 = f32[256,256]{1,0:T(8,128)} copy(f32[256,256]{1,0:T(8,128)S(1)} %shard_map.109) | data formatting | bytes 524288
